TPU v7x, 128 devices: a whole 4x4x4 slice. The times are simulated.
128 devices in a mesh: ctx: 32 (over z, y, core), exp: 4 (over x).
Axes of the slice: x: 4, y: 4, z: 4, core: 2. Of those that a mesh axis runs over, the one named last changes fastest.
Arguments:
- projected: bfloat16 [3, 8192, 4096], P(None, 'ctx', 'exp'), may hold values from -6 to 6
- short_filter: float32 [3, 3, 4096], P(None, None, 'exp'), may hold values from -3.5 to 3.5
- long_filter: float32 [128, 4096], P(None, 'exp'), may hold values from -0.5 to 0.5
- residual_in: bfloat16 [8192, 4096], P('ctx', 'exp'), may hold values from -16 to 16
- norm_gain: float32 [4096], replicated, may hold values from 0.1 to 1.9
- expert_ids: int32 [8192], P('ctx'), may hold values from 0 to 15, as said below
- gate_weight: bfloat16 [32, 4096, 3072], P('ctx', None, 'exp'), may hold values from -0.09375 to 0.09375
- up_weight: bfloat16 [32, 4096, 3072], P('ctx', None, 'exp'), may hold values from -0.09375 to 0.09375
- down_weight: bfloat16 [32, 3072, 4096], P('ctx', 'exp'), may hold values from -0.078125 to 0.078125
Outputs:
- out: bfloat16 [8192, 4096], P('ctx', 'exp')
Inputs may be any that keep to these rules, and one draw needn't show every extreme that they name: `expert_ids`: among the 256 positions of each device no expert is named more than 40 times; one expert, the same on all devices, is named exactly 40 times on every device.
All inputs are finite; a program needn't handle non-finite values.
Results may differ from a plain program's by a relative error of at most 0.008.
Values may be sent and summed in bfloat16 or wider, within the bound.
No kernel may reach another device: no remote copies, remote signals or barrier semaphores. Data moves between devices by JAX's collectives and lax.ppermute only.
A program may use at most 128 MiB of HBM per device.

v0:
```python
import jax
import jax.numpy as jnp
from jax import lax
from jax.sharding import PartitionSpec as P


def passed_along(block, axis, distance):
    devices = range(lax.axis_size(axis))
    route = [(i - distance, i) for i in devices if i - distance in devices]
    return lax.ppermute(block, axis, route)


def short_conv(extended, kernel):
    short_len = kernel.shape[0]
    length = extended.shape[0] - (short_len - 1)
    values = extended.astype(jnp.float32)
    total = jnp.zeros((length, extended.shape[1]), jnp.float32)
    for offset in range(short_len):
        total = (
            total
            + kernel[offset] * values[short_len - 1 - offset : short_len - 1 - offset + length]
        )
    return total


def long_conv(product, long_filter):
    channels = product.shape[1]
    lhs = product.astype(jnp.float32)[None]
    rhs = long_filter[::-1][:, None, :]
    result = lax.conv_general_dilated(
        lhs,
        rhs,
        (1,),
        "VALID",
        dimension_numbers=("NWC", "WIO", "NWC"),
        feature_group_count=channels,
        precision=lax.Precision.HIGHEST,
    )
    return result[0]


def build_send(normed, slot_token):
    padded = jnp.concatenate([normed, jnp.zeros((1, normed.shape[1]), normed.dtype)], axis=0)
    by_expert = padded[slot_token]
    return jnp.repeat(by_expert, 2, axis=0)


def body(
    projected,
    short_filter,
    long_filter,
    residual_in,
    norm_gain,
    expert_ids,
    gate_weight,
    up_weight,
    down_weight,
):
    tok_rows = projected.shape[1]
    tap_count = long_filter.shape[0]
    short_len = short_filter.shape[1]
    halves = lax.axis_size("ctx")
    experts = halves // 2
    capacity = 5 * tok_rows // halves
    tail_rows = tap_count + short_len - 2
    prev_pair, previous_query = passed_along(
        (projected[1:, tok_rows - tail_rows :, :], projected[0, tok_rows - (short_len - 1) :, :]),
        "ctx",
        1,
    )
    key_s = short_conv(jnp.concatenate([prev_pair[0], projected[1]], axis=0), short_filter[1])
    value_s = short_conv(jnp.concatenate([prev_pair[1], projected[2]], axis=0), short_filter[2])
    product = (key_s * value_s).astype(jnp.bfloat16)
    query_s = short_conv(jnp.concatenate([previous_query, projected[0]], axis=0), short_filter[0])
    long_out = long_conv(product, long_filter)
    h_state = (residual_in.astype(jnp.float32) + query_s * long_out).astype(jnp.bfloat16)
    one_hot = (expert_ids[:, None] == jnp.arange(experts, dtype=jnp.int32)[None, :]).astype(
        jnp.int32
    )
    earlier = jnp.cumsum(one_hot, axis=0) - one_hot
    position = jnp.sum(earlier * one_hot, axis=1)
    slot_token = (
        jnp.full((experts, capacity), tok_rows, jnp.int32)
        .at[expert_ids, position]
        .set(jnp.arange(tok_rows, dtype=jnp.int32))
    )
    w_gate = gate_weight[0]
    w_up = up_weight[0]
    w_down = down_weight[0]
    full_rows = lax.all_gather(h_state, "exp", axis=1, tiled=True)
    full_float = full_rows.astype(jnp.float32)
    scale = lax.rsqrt(jnp.mean(full_float * full_float, axis=1, keepdims=True) + 1e-06)
    normed = (full_float * scale * norm_gain[None, :]).astype(jnp.bfloat16)
    received = lax.all_to_all(
        build_send(normed, slot_token), "ctx", split_axis=0, concat_axis=0, tiled=True
    )
    flat_rows = received.reshape(halves * capacity, received.shape[2])
    gate_pre = jnp.dot(flat_rows, w_gate, preferred_element_type=jnp.float32)
    up_pre = jnp.dot(flat_rows, w_up, preferred_element_type=jnp.float32)
    hidden = (jax.nn.silu(gate_pre) * up_pre).astype(jnp.bfloat16)
    term = jnp.dot(hidden, w_down, preferred_element_type=jnp.float32)
    rounded = lax.optimization_barrier(term.astype(jnp.bfloat16))
    full_width = rounded.shape[1]
    returned = lax.all_to_all(
        rounded.reshape(halves, capacity, full_width),
        "ctx",
        split_axis=0,
        concat_axis=0,
        tiled=True,
    )
    paired = returned[2 * expert_ids, position].astype(jnp.float32) + returned[
        2 * expert_ids + 1, position
    ].astype(jnp.float32)
    moe = lax.psum_scatter(
        paired.astype(jnp.bfloat16), "exp", scatter_dimension=1, tiled=True
    ).astype(jnp.float32)
    return (h_state.astype(jnp.float32) + moe).astype(jnp.bfloat16)


def solution(mesh):
    return jax.shard_map(
        body,
        mesh=mesh,
        in_specs=(
            P(None, "ctx", "exp"),
            P(None, None, "exp"),
            P(None, "exp"),
            P("ctx", "exp"),
            P(),
            P("ctx"),
            P("ctx", None, "exp"),
            P("ctx", None, "exp"),
            P("ctx", "exp", None),
        ),
        out_specs=P("ctx", "exp"),
        check_vma=False,
    )
```

profile of v0, /device:TPU:6, one launch (start us, length us, event | category | flops | bytes accessed | tf_op | source)
XLA Modules:
  0.0 418.3 jit_solution(12293649097460453306)
XLA Ops:
  6.5 0.0 all-gather.2.cloned.1.call-start
  6.5 0.7 slice_bitcast_fusion.5
  7.3 0.0 copy-start.5
  7.3 0.0 copy-start.3
  7.3 1.9 collective-permute-start
  9.2 1.2 slice.111
  10.4 3.8 collective-permute-start.1
  14.2 1.5 slice_bitcast_fusion.1
  15.6 0.0 copy-done.5
  15.7 0.0 copy-done.3
  15.7 2.6 rev.3
  18.3 0.0 collective-permute-done
  18.3 0.1 maximum_convert_fusion.2
  18.5 0.0 collective-permute-done.1
  18.5 0.4 maximum_convert_fusion
  19.0 0.0 copy-start.4
  19.0 1.0 fusion.27
  20.0 0.0 copy-done.4
  20.0 0.0 copy-start.2
  20.0 10.7 %fusion.20 = f32[1,256,1024]{2,0,1:T(1,128)S(1)} fusion(bf16[1,383,1024]{2,1,0:T(8,128)(2,1)S(1)} %fusion.27, f32[128,1,1024]{2,0,1:T(8,128)S(1)} %bitcast.82), kind=kOutput, calls=%fused_computation.30 | convolution fusion | flops 402653184 | bytes 2357248 | tf_op jit(solution)/shard_map/conv_general_dilated | solution.py:30
  30.8 0.0 copy-done.2
  30.8 0.0 copy-start.7
  30.8 1.3 fusion.25
  32.1 0.0 all-gather.2.cloned.1.call-update
  32.1 0.0 reduce-scatter.2.cloned.1.call-start
  32.2 0.0 copy-done.7
  32.2 0.6 reduce-window.6
  32.8 0.2 slice_reduce_fusion
  33.0 0.1 fusion.31
  33.1 0.0 copy-start.6
  33.2 12.8 %scatter_fusion = s32[16,40]{1,0:T(8,128)S(1)} fusion(s32[16,40]{1,0:T(8,128)S(1)} %broadcast_in_dim.34, s32[256]{0:T(256)S(1)} %bitcast.78, s32[256]{0:T(256)S(1)} %iota.11), kind=kCustom, calls=%fused_computation.3 | custom fusion | bytes 5120 | tf_op jit(solution)/shard_map/scatter | solution.py:85
  45.9 0.1 reshape.71
  46.0 20.4 %all-gather.2.cloned.1.call-done = bf16[256,4096]{1,0:T(8,128)(2,1)} async-done(((bf16[256,1024]{1,0:T(8,128)(2,1)}), bf16[256,4096]{1,0:T(8,128)(2,1)}) %all-gather.2.cloned.1.call-update) | async-done | bytes 2097168 | tf_op jit(solution)/shard_map/all_gather | solution.py:90
  66.4 0.0 copy-start
  66.4 2.2 fusion.8
  68.7 0.0 copy-done.6
  68.7 0.0 copy-done
  68.7 0.6 fusion.10
  69.3 0.3 concatenate.24
  69.6 5.4 %gather_fusion = bf16[640,4096]{1,0:T(8,128)(2,1)} fusion(bf16[257,4096]{1,0:T(8,128)(2,1)S(1)} %concatenate.24, s32[1024]{0:T(1024)S(1)} %pad_clamp_fusion), kind=kCustom, calls=%fused_computation | custom fusion | bytes 10488320 | tf_op jit(solution)/shard_map/gather | solution.py:44
  75.0 7.9 %broadcast_in_dim.37 = bf16[16,2,40,4096]{3,2,1,0:T(8,128)(2,1)} broadcast(bf16[16,40,4096]{2,1,0:T(8,128)(2,1)} %bitcast.75), dimensions={0,2,3} | broadcast | bytes 15728640 | tf_op jit(solution)/shard_map/broadcast_in_dim | solution.py:45
  82.9 0.0 slice-start
  82.9 0.0 slice-start.2
  82.9 126.0 %all_to_all.10 = bf16[32,40,4096]{2,1,0:T(8,128)(2,1)S(1)} all-to-all(bf16[32,40,4096]{2,1,0:T(8,128)(2,1)} %bitcast.74), channel_id=1, replica_groups=mesh['ctx'=32,'exp'=4] {'ctx'}, dimensions={0} | all-to-all | bytes 20971520 | tf_op jit(solution)/shard_map/all_to_all | solution.py:94
  208.9 0.0 slice-start.1
  208.9 0.0 slice-start.3
  208.9 11.8 %fusion.3 = f32[1280,768]{1,0:T(8,128)} fusion(bf16[1280,4096]{1,0:T(8,128)(2,1)S(1)} %bitcast.79, bf16[1,4096,768]{2,1,0:T(8,128)(2,1)} %param.15), kind=kOutput, calls=%fused_computation.8 | convolution fusion | flops 8053063680 | bytes 20709376 | tf_op jit(solution)/shard_map/dot_general | solution.py:98
  220.7 0.0 slice-done
  220.7 0.0 slice-done.1
  220.7 10.3 %fusion.11 = bf16[1280,768]{1,0:T(8,128)(2,1)S(1)} fusion(bf16[1280,4096]{1,0:T(8,128)(2,1)S(1)} %bitcast.80, bf16[1,4096,768]{2,1,0:T(8,128)(2,1)S(1)} %bitcast.98, f32[1280,768]{1,0:T(8,128)} %fusion.3), kind=kOutput, calls=%fused_computation.17 | convolution fusion | flops 8058961920 | bytes 22675456 | tf_op jit(solution)/shard_map/dot_general | solution.py:99
  231.0 0.0 slice-done.2
  231.0 0.0 slice-done.3
  231.0 8.9 %convolution_convert_fusion = bf16[1280,4096]{1,0:T(8,128)(2,1)S(1)} fusion(bf16[1280,768]{1,0:T(8,128)(2,1)S(1)} %fusion.11, bf16[1,768,4096]{2,1,0:T(8,128)(2,1)S(1)} %bitcast.100), kind=kOutput, calls=%fused_computation.4 | convolution fusion | flops 8058306560 | bytes 18743296 | tf_op jit(solution)/shard_map/dot_general | solution.py:101
  239.9 123.8 %all_to_all.11 = bf16[32,40,4096]{2,1,0:T(8,128)(2,1)} all-to-all(bf16[32,40,4096]{2,1,0:T(8,128)(2,1)S(1)} %bitcast.81), channel_id=1, replica_groups=mesh['ctx'=32,'exp'=4] {'ctx'}, dimensions={0} | all-to-all | bytes 20971520 | tf_op jit(solution)/shard_map/all_to_all | solution.py:104
  363.8 6.1 %gather_fusion.2 = bf16[256,4096]{1,0:T(8,128)(2,1)S(1)} fusion(bf16[32,40,4096]{2,1,0:T(8,128)(2,1)} %all_to_all.11, s32[256]{0:T(256)S(1)} %bitcast.77), kind=kCustom, calls=%fused_computation.2 | custom fusion | bytes 4196352 | tf_op jit(solution)/shard_map/gather | solution.py:111
  369.9 7.5 %gather_fusion.1 = bf16[256,4096]{1,0:T(8,128)(2,1)} fusion(bf16[32,40,4096]{2,1,0:T(8,128)(2,1)} %all_to_all.11, s32[256]{0:T(256)S(1)} %bitcast.76), kind=kCustom, calls=%fused_computation.1 | custom fusion | bytes 4196352 | tf_op jit(solution)/shard_map/gather | solution.py:111
  377.4 3.7 add_convert_fusion
  381.1 0.0 copy-start.1
  381.1 0.0 reduce-scatter.2.cloned.1.call-update
  381.1 28.4 %reduce-scatter.2.cloned.1.call-done = bf16[256,1024]{1,0:T(8,128)(2,1)} async-done(((bf16[256,4096]{1,0:T(8,128)(2,1)}), bf16[256,1024]{1,0:T(8,128)(2,1)}) %reduce-scatter.2.cloned.1.call-update) | async-done | bytes 524304 | tf_op jit(solution)/shard_map/reduce_scatter | solution.py:114
  409.5 0.0 copy-done.1
  409.5 2.0 add_convert_fusion.1
  (14 shorter events, 0.2 us)
Async XLA Ops:
  6.5 59.9 %all-gather.2.cloned.1.call-start = ((), (), s32[]{:S(2)}) async-start(), calls=%async_computation.3 | async-start | bytes 2621440 | tf_op jit(solution)/shard_map/all_gather | solution.py:90
  7.3 8.4 %copy-start.5 = (f32[3,3,1024]{2,1,0:T(4,128)S(1)}, f32[3,3,1024]{2,1,0:T(4,128)}, u32[]{:S(2)}) copy-start(f32[3,3,1024]{2,1,0:T(4,128)} %param.10) | copy-start | bytes 110596
  7.3 8.4 %copy-start.3 = (f32[128,1024]{1,0:T(8,128)S(1)}, f32[128,1024]{1,0:T(8,128)}, u32[]{:S(2)}) copy-start(f32[128,1024]{1,0:T(8,128)} %param.11) | copy-start | bytes 1572868
  7.3 11.1 %collective-permute-start = (bf16[2,1024]{1,0:T(2,128)(2,1)S(1)}, bf16[2,1024]{1,0:T(2,128)(2,1)S(1)}, u32[]{:S(2)}, u32[]{:S(2)}) collective-permute-start(bf16[2,1024]{1,0:T(2,128)(2,1)S(1)} %slice_bitcast_fusion.5), channel_id=1, source_target_pairs={{0,4},{4,8},{8,12},{12,16},{16,20},{20,24},{24,28},{28,32},{32,36}... | collective-permute-start | bytes 12296 | tf_op jit(solution)/shard_map/ppermute | solution.py:10
  10.4 8.1 %collective-permute-start.1 = (bf16[2,129,1024]{2,1,0:T(8,128)(2,1)S(1)}, bf16[2,129,1024]{2,1,0:T(8,128)(2,1)S(1)}, u32[]{:S(2)}, u32[]{:S(2)}) collective-permute-start(bf16[2,129,1024]{2,1,0:T(8,128)(2,1)S(1)} %slice.111), channel_id=1, source_target_pairs={{0,4},{4,8},{8,12},{12,16},{16,20},{20,24},{24,28},{28,32},{32,36}... | collective-permute-start | bytes 1585160 | tf_op jit(solution)/shard_map/ppermute | solution.py:10
  19.0 1.0 copy-start.4
  20.0 10.8 %copy-start.2 = (bf16[256,1024]{1,0:T(8,128)(2,1)S(1)}, bf16[256,1024]{1,0:T(8,128)(2,1)}, u32[]{:S(2)}) copy-start(bf16[256,1024]{1,0:T(8,128)(2,1)} %param.12) | copy-start | bytes 1572868
  30.8 1.4 copy-start.7
  32.1 377.4 %reduce-scatter.2.cloned.1.call-start = ((), (), s32[]{:S(2)}) async-start(), calls=%async_computation.4 | async-start | bytes 2621440 | tf_op jit(solution)/shard_map/reduce_scatter | solution.py:114
  33.1 35.5 %copy-start.6 = (f32[4096]{0:T(1024)S(1)}, f32[4096]{0:T(1024)}, u32[]{:S(2)}) copy-start(f32[4096]{0:T(1024)} %param.13) | copy-start | bytes 49156
  66.4 2.3 copy-start
  82.9 137.8 %slice-start = ((s8[6291456]{0:T(1024)(128)(4,1)}), s8[4194304]{0:T(1024)(128)(4,1)S(1)}, s32[]{:S(2)}) async-start(s8[6291456]{0:T(1024)(128)(4,1)} %bitcast.97), calls=%async_computation.5 | async-start | bytes 8388608
  82.9 148.1 %slice-start.2 = ((s8[6291456]{0:T(1024)(128)(4,1)}), s8[4194304]{0:T(1024)(128)(4,1)S(1)}, s32[]{:S(2)}) async-start(s8[6291456]{0:T(1024)(128)(4,1)} %bitcast.99), calls=%async_computation.7 | async-start | bytes 8388608
  208.9 11.9 %slice-start.1 = ((s8[6291456]{0:T(1024)(128)(4,1)}), s8[2097152]{0:T(1024)(128)(4,1)S(1)}, s32[]{:S(2)}) async-start(s8[6291456]{0:T(1024)(128)(4,1)} %bitcast.97), calls=%async_computation.6 | async-start | bytes 4194304
  208.9 22.2 %slice-start.3 = ((s8[6291456]{0:T(1024)(128)(4,1)}), s8[2097152]{0:T(1024)(128)(4,1)S(1)}, s32[]{:S(2)}) async-start(s8[6291456]{0:T(1024)(128)(4,1)} %bitcast.99), calls=%async_computation.8 | async-start | bytes 4194304
  381.1 28.4 %copy-start.1 = (bf16[256,1024]{1,0:T(8,128)(2,1)S(1)}, bf16[256,1024]{1,0:T(8,128)(2,1)}, u32[]{:S(2)}) copy-start(bf16[256,1024]{1,0:T(8,128)(2,1)} %fusion.25) | copy-start | bytes 1572868
Sparse Core Ops, SparseCore 0:
  32.2 34.1 all-gather.1
  381.2 28.1 reduce-scatter.1
where the time goes:
time: 422 us; the launch traced here: 418 us
  blocking collectives  250 us (59%)
  waiting for transfers between devices  48.8 us (12%)
  local copies, waits for them, and re-layouts  46.3 us (11%)
  matrix products  41.8 us (10%)
  between operations  13.7 us (3%)
  other arithmetic  12.2 us (3%)
  starting transfers between devices  5.71 us (1%)
    all_to_all x1, blocking collectives, body(): lax.all_to_all(build_send(normed, slot_token), 'ctx', split_axis=0, conca...  126 us
    all_to_all x1, blocking collectives, body(): lax.all_to_all(rounded.reshape(halves, capacity, full_width), 'ctx', spli...  124 us
    reduce_scatter x1, waiting for transfers between devices, body(): lax.psum_scatter(paired.astype(jnp.bfloat16), 'exp', scatter_dimension=1,...  28.4 us
    all_gather x1, waiting for transfers between devices, body(): full_rows = lax.all_gather(h_state, 'exp', axis=1, tiled=True)  20.4 us
    scatter x1, local copies, waits for them, and re-layouts, body(): slot_token = jnp.full((experts, capacity), tok_rows, jnp.int32).at[expert...  12.8 us
    dot_general x1, matrix products, body(): gate_pre = jnp.dot(flat_rows, w_gate, preferred_element_type=jnp.float32)  11.8 us
    conv_general_dilated x1, matrix products, long_conv(): lax.conv_general_dilated(lhs, rhs, (1,), 'VALID', dimension_numbers=('NWC...  10.7 us
    dot_general x1, matrix products, body(): up_pre = jnp.dot(flat_rows, w_up, preferred_element_type=jnp.float32)  10.3 us
  transfers between devices with their start and end apart: 4, of which 2 were waited for; matrix products, arithmetic and copies ran while one was open for 5% of the time, Pallas kernels for 0%

commit v1 on v0

v1 whole, which is shorter than its diff:
```python
import functools

import jax
import jax.numpy as jnp
import numpy as np
from jax import lax
from jax.experimental import pallas as pl
from jax.experimental.pallas import tpu as pltpu
from jax.sharding import Mesh
from jax.sharding import PartitionSpec as P

D = 4096
TAPS = 128
TOK = 256
QUARTER = 1024
HID = 768
EXPERTS = 16
CAP = 40
SLOTS = EXPERTS * CAP
SPAN = TOK + TAPS
BINS = 200
HALO = 144
QHALO = 16
LANES = 256
HALF = 320
ROWS = 2 * HALF
VMEM = 100 << 19


def dft_matrices():
    n = np.arange(SPAN)
    k = np.arange(BINS)
    angle = 2 * np.pi * ((k[:, None] * n[None, :]) % SPAN) / SPAN
    live = (k <= SPAN // 2)[:, None]
    forward = np.concatenate([np.cos(angle) * live, -np.sin(angle) * live], axis=0)
    weight = np.where((k == 0) | (k == SPAN // 2), 1.0, 2.0) * (k <= SPAN // 2) / SPAN
    back = np.concatenate(
        [np.cos(angle).T[TAPS:] * weight, -np.sin(angle).T[TAPS:] * weight], axis=1
    )
    return forward.astype(np.float32), back.astype(np.float32)


def split(value, parts):
    out = []
    rest = value
    for _ in range(parts):
        piece = rest.astype(jnp.bfloat16)
        out.append(piece)
        rest = rest - piece.astype(jnp.float32)
    return out


def split_np(value, parts):
    out = []
    rest = value
    for _ in range(parts):
        piece = rest.astype(jnp.bfloat16)
        out.append(piece)
        rest = rest - piece.astype(np.float32)
    return out


def mm(a, b):
    return jnp.dot(a, b, preferred_element_type=jnp.float32)


def slots_of(ids_col, ids_row, axis):
    first = lax.broadcasted_iota(jnp.int32, (TOK, TOK), 0)
    second = lax.broadcasted_iota(jnp.int32, (TOK, TOK), 1)
    same = ids_col == ids_row
    earlier = (first < second) if axis == 0 else (second < first)
    rank = jnp.sum(jnp.where(same & earlier, 1.0, 0.0), axis=axis, keepdims=True)
    ids = ids_row if axis == 0 else ids_col
    return ids * CAP + rank.astype(jnp.int32)


def taps3(ext, filt, start, length):
    return (
        filt[0:1] * ext[start : start + length]
        + filt[1:2] * ext[start - 1 : start - 1 + length]
        + filt[2:3] * ext[start - 2 : start - 2 + length]
    )


def front_kernel(
    x_ref, proj, halo_kv, halo_q, short, long_f, res, gain, ids_col, ids_row,
    fwd1, fwd2, fwd3, back1, back2, back3, h_out, send_out,
):
    f32 = jnp.float32

    def extended(halo, body):
        return jnp.concatenate([halo.astype(f32), body.astype(f32)], axis=0)

    s1 = taps3(extended(halo_kv[0], proj[1]), short[1], HALO - TAPS, SPAN)
    s2 = taps3(extended(halo_kv[1], proj[2]), short[2], HALO - TAPS, SPAN)
    s0 = taps3(extended(halo_q[...], proj[0]), short[0], QHALO, TOK)
    kv = (s1 * s2).astype(jnp.bfloat16)
    spec = mm(fwd1[...], kv) + mm(fwd2[...], kv) + mm(fwd3[...], kv)
    f1, f2, f3 = split(long_f[...], 3)
    a1, a2, a3 = fwd1[:, :TAPS], fwd2[:, :TAPS], fwd3[:, :TAPS]
    filt = mm(a1, f1) + (mm(a1, f2) + mm(a2, f1)) + (mm(a1, f3) + mm(a2, f2) + mm(a3, f1))
    re, im = spec[:BINS], spec[BINS:]
    fre, fim = filt[:BINS], filt[BINS:]
    prod = jnp.concatenate([re * fre - im * fim, re * fim + im * fre], axis=0)
    p1, p2, p3 = split(prod, 3)
    b1, b2, b3 = back1[...], back2[...], back3[...]
    long_out = mm(b1, p1) + (mm(b1, p2) + mm(b2, p1)) + (mm(b1, p3) + mm(b2, p2) + mm(b3, p1))
    h = (res[...].astype(f32) + s0 * long_out).astype(jnp.bfloat16)
    h_out[...] = h
    gained = (h.astype(f32) * gain[...]).astype(jnp.bfloat16)
    slot_row = slots_of(ids_col[...], ids_row[...], 0)
    slot = lax.broadcasted_iota(jnp.int32, (SLOTS, TOK), 0)
    pick = jnp.where(slot == slot_row, 1.0, 0.0).astype(jnp.bfloat16)
    send_out[...] = mm(pick, gained).astype(jnp.bfloat16)


def front(x_at, projected, halo_kv, halo_q, short, long_f, res, gain, ids):
    forward, back = dft_matrices()
    fwd = [jnp.asarray(p) for p in split_np(forward, 3)]
    bck = [jnp.asarray(p) for p in split_np(back, 3)]
    steps = QUARTER // LANES

    def whole(shape):
        return pl.BlockSpec(shape, lambda i, x: (0,) * len(shape))

    in_specs = [
        pl.BlockSpec((3, TOK, LANES), lambda i, x: (0, 0, i)),
        pl.BlockSpec((2, HALO, LANES), lambda i, x: (0, 0, i)),
        pl.BlockSpec((QHALO, LANES), lambda i, x: (0, i)),
        pl.BlockSpec((3, 3, LANES), lambda i, x: (0, 0, i)),
        pl.BlockSpec((TAPS, LANES), lambda i, x: (0, i)),
        pl.BlockSpec((TOK, LANES), lambda i, x: (0, i)),
        pl.BlockSpec((1, LANES), lambda i, x: (0, x[0] * steps + i)),
        whole((TOK, 1)),
        whole((1, TOK)),
    ]
    in_specs += [whole((2 * BINS, SPAN))] * 3 + [whole((TOK, 2 * BINS))] * 3
    return pl.pallas_call(
        front_kernel,
        grid_spec=pltpu.PrefetchScalarGridSpec(
            num_scalar_prefetch=1,
            grid=(steps,),
            in_specs=in_specs,
            out_specs=[
                pl.BlockSpec((TOK, LANES), lambda i, x: (0, i)),
                pl.BlockSpec((SLOTS, LANES), lambda i, x: (0, i)),
            ],
        ),
        out_shape=[
            jax.ShapeDtypeStruct((TOK, QUARTER), jnp.bfloat16),
            jax.ShapeDtypeStruct((SLOTS, QUARTER), jnp.bfloat16),
        ],
        compiler_params=pltpu.CompilerParams(vmem_limit_bytes=VMEM),
        name="front",
    )(
        x_at, projected, halo_kv, halo_q, short, long_f, res, gain.reshape(1, D),
        ids.reshape(TOK, 1), ids.reshape(1, TOK), *fwd, *bck,
    )


PIECES = ((0, 0, HALF), (1, 0, HALF), (2, 0, HALF), (3, 0, HALF // 2), (3, HALF // 2, HALF // 2))


def expert_kernel(x_ref, *refs):
    pieces = refs[:10]
    wg, wu, wd, ig, own_out, sib_out, xs, accg, accu, ssq, hid, sems = refs[10:]
    i = pl.program_id(0)
    copies = []
    for core in range(2):
        for n, (block, start, rows) in enumerate(PIECES):
            at = core * 5 + n
            copies.append(
                (
                    block,
                    pltpu.make_async_copy(
                        pieces[at],
                        xs.at[block, pl.ds(core * HALF + start, rows)],
                        sems.at[at],
                    ),
                )
            )

    @pl.when(i == 0)
    def _():
        for _, copy in sorted(copies, key=lambda c: c[0]):
            copy.start()

    for k in range(4):

        @pl.when(i == k)
        def _():
            for block, copy in copies:
                if block == k:
                    copy.wait()
            xk = xs[k]
            g = mm(xk, wg[...])
            u = mm(xk, wu[...])
            h = xk.astype(jnp.float32) * ig[0]
            sq = h * h
            part = sq[:, 0:128]
            for c in range(1, QUARTER // 128):
                part = part + sq[:, c * 128 : (c + 1) * 128]
            if k == 0:
                accg[...] = g
                accu[...] = u
                ssq[...] = part
            elif k < 3:
                accg[...] += g
                accu[...] += u
                ssq[...] += part
            else:
                total = jnp.sum(ssq[...] + part, axis=1, keepdims=True)
                scale = lax.rsqrt(total / D + 1e-06)
                gate = (accg[...] + g) * scale
                up = (accu[...] + u) * scale
                hid[...] = (gate / (1.0 + jnp.exp(-gate)) * up).astype(jnp.bfloat16)

    @pl.when(i >= 4)
    def _():
        y = mm(hid[...], wd[...]).astype(jnp.bfloat16)
        own_out[0] = y[:HALF]
        sib_out[0] = y[HALF:]


def expert(x_at, pieces, wg, wu, wd, inv_gain):
    def k_block(i, x):
        k = jnp.minimum(i, 3)
        off = jnp.where(k == 1, 3, jnp.where(k == 0, 0, k - 1))
        return lax.rem(x[0] + off, 4)

    def n_block(i, x):
        j = jnp.maximum(i - 4, 0)
        off = jnp.where(j == 0, 2, jnp.where(j == 1, 1, jnp.where(j == 2, 3, 0)))
        return lax.rem(x[0] + off, 4)

    any_spec = pl.BlockSpec(memory_space=pl.ANY)
    out_spec = pl.BlockSpec((1, HALF, QUARTER), lambda i, x: (jnp.maximum(i - 4, 0), 0, 0))
    out_type = jax.ShapeDtypeStruct((4, HALF, QUARTER), jnp.bfloat16)
    return pl.pallas_call(
        expert_kernel,
        grid_spec=pltpu.PrefetchScalarGridSpec(
            num_scalar_prefetch=1,
            grid=(8,),
            in_specs=[any_spec] * 10
            + [
                pl.BlockSpec((QUARTER, HID), lambda i, x: (k_block(i, x), 0)),
                pl.BlockSpec((QUARTER, HID), lambda i, x: (k_block(i, x), 0)),
                pl.BlockSpec((HID, QUARTER), lambda i, x: (0, n_block(i, x))),
                pl.BlockSpec((1, 1, QUARTER), lambda i, x: (k_block(i, x), 0, 0)),
            ],
            out_specs=[out_spec, out_spec],
            scratch_shapes=[
                pltpu.VMEM((4, ROWS, QUARTER), jnp.bfloat16),
                pltpu.VMEM((ROWS, HID), jnp.float32),
                pltpu.VMEM((ROWS, HID), jnp.float32),
                pltpu.VMEM((ROWS, 128), jnp.float32),
                pltpu.VMEM((ROWS, HID), jnp.bfloat16),
                pltpu.SemaphoreType.DMA((10,)),
            ],
        ),
        out_shape=[out_type, out_type],
        compiler_params=pltpu.CompilerParams(vmem_limit_bytes=VMEM),
        cost_estimate=pl.CostEstimate(
            flops=2 * 3 * ROWS * D * HID, bytes_accessed=32 << 20, transcendentals=ROWS * HID
        ),
        name="expert",
    )(x_at, *pieces, wg, wu, wd, inv_gain)


def finish_kernel(h, back, ids_col, ids_row, out):
    slot_col = slots_of(ids_col[...], ids_row[...], 1)
    slot = lax.broadcasted_iota(jnp.int32, (TOK, SLOTS), 1)
    pick = jnp.where(slot == slot_col, 1.0, 0.0).astype(jnp.bfloat16)
    moe = mm(pick, back[...])
    out[...] = (h[...].astype(jnp.float32) + moe).astype(jnp.bfloat16)


def finish(h, back, ids):
    return pl.pallas_call(
        finish_kernel,
        grid=(QUARTER // LANES,),
        in_specs=[
            pl.BlockSpec((TOK, LANES), lambda i: (0, i)),
            pl.BlockSpec((SLOTS, LANES), lambda i: (0, i)),
            pl.BlockSpec((TOK, 1), lambda i: (0, 0)),
            pl.BlockSpec((1, TOK), lambda i: (0, 0)),
        ],
        out_specs=pl.BlockSpec((TOK, LANES), lambda i: (0, i)),
        out_shape=jax.ShapeDtypeStruct((TOK, QUARTER), jnp.bfloat16),
        compiler_params=pltpu.CompilerParams(vmem_limit_bytes=VMEM),
        name="finish",
    )(h, back, ids.reshape(TOK, 1), ids.reshape(1, TOK))


def along_x(block, step):
    return lax.ppermute(block, "x", [(i, (i + step) % 4) for i in range(4)])


def other_core(block):
    return lax.ppermute(block, "c", [(0, 1), (1, 0)])


def add(*terms):
    total = terms[0].astype(jnp.float32)
    for term in terms[1:]:
        total = total + term.astype(jnp.float32)
    return total.astype(jnp.bfloat16)


def gather_x(own):
    mid = HALF // 2
    left = along_x(own, 1)
    right = along_x(own, -1)
    far_a = along_x(left[:mid], 1)
    far_b = along_x(right[mid:], -1)
    mine = [own, left, right, far_a, far_b]
    return mine + [other_core(piece) for piece in mine]


def scatter_x(own_out, sib_out):
    mid = HALF // 2
    far, right, left, here = [add(own_out[j], other_core(sib_out[j])) for j in range(4)]
    via_left = along_x(far[:mid], 1)
    via_right = along_x(far[mid:], -1)
    to_right = jnp.concatenate([add(right[:mid], via_left), right[mid:]], axis=0)
    to_left = jnp.concatenate([left[:mid], add(left[mid:], via_right)], axis=0)
    from_left = along_x(to_right, 1)
    from_right = along_x(to_left, -1)
    return add(here, from_left, from_right)


def body(
    projected, short_filter, long_filter, residual_in, norm_gain, expert_ids,
    gate_weight, up_weight, down_weight,
):
    x_at = lax.axis_index("x").astype(jnp.int32).reshape(1)
    route = [(i, i + 1) for i in range(31)]
    halo_kv = lax.ppermute(projected[1:, TOK - HALO :, :], ("z", "y", "c"), route)
    halo_q = lax.ppermute(projected[0, TOK - QHALO :, :], ("z", "y", "c"), route)
    h, send = front(
        x_at, projected, halo_kv, halo_q, short_filter, long_filter, residual_in,
        norm_gain, expert_ids,
    )
    got = lax.all_to_all(
        send.reshape(EXPERTS, CAP, QUARTER), ("z", "y"), split_axis=0, concat_axis=0, tiled=True
    ).reshape(SLOTS, QUARTER)
    inv_gain = (1.0 / norm_gain).reshape(4, 1, QUARTER)
    weights = (gate_weight[0], up_weight[0], down_weight[0])
    done = []
    for part in range(2):
        pieces = gather_x(got[part * HALF : (part + 1) * HALF])
        own_out, sib_out = expert(x_at, pieces, *weights, inv_gain)
        done.append(scatter_x(own_out, sib_out))
    back = lax.all_to_all(
        jnp.concatenate(done, axis=0).reshape(EXPERTS, CAP, QUARTER),
        ("z", "y"), split_axis=0, concat_axis=0, tiled=True,
    ).reshape(SLOTS, QUARTER)
    return finish(h, back, expert_ids)


def solution(mesh):
    grid = Mesh(mesh.devices.reshape(4, 4, 2, 4), ("z", "y", "c", "x"))
    ctx = ("z", "y", "c")
    return jax.shard_map(
        body,
        mesh=grid,
        in_specs=(
            P(None, ctx, "x"),
            P(None, None, "x"),
            P(None, "x"),
            P(ctx, "x"),
            P(),
            P(ctx),
            P(ctx, None, "x"),
            P(ctx, None, "x"),
            P(ctx, "x", None),
        ),
        out_specs=P(ctx, "x"),
        check_vma=False,
    )
```

time: 422 us -> 232 us (0.55)
  blocking collectives: 250 us -> 52.1 us
  Pallas kernels: 0 us -> 55.7 us
  matrix products: 41.8 us -> 0 us
  local copies, waits for them, and re-layouts: 46.3 us -> 14.7 us
  waiting for transfers between devices: 48.8 us -> 75.3 us
  starting transfers between devices: 5.71 us -> 29.4 us
  between operations: 13.7 us -> 0.47 us
  other arithmetic: 12.2 us -> 3.45 us
    all_to_all x2, blocking collectives: 250 us -> 52.1 us  [the longest x1 31.6 us: body(): lax.all_to_all(send.reshape(EXPERTS, CAP, QUARTER), ('z', 'y'), split_axi...]
    ppermute x2 -> x36, waiting for transfers between devices: 0.01 us -> 75.3 us  [the longest x16 74.7 us: along_x(): return lax.ppermute(block, 'x', [(i, (i + step) % 4) for i in range(4)])]
    pallas_call x0 -> x4, Pallas kernels: none -> 55.7 us  [the longest x2 40.2 us: expert(): pl.pallas_call(expert_kernel, grid_spec=pltpu.PrefetchScalarGridSpec(num_...]
    dot_general x3 -> x0, matrix products: 31 us -> none  [the longest x1 11.8 us: body(): gate_pre = jnp.dot(flat_rows, w_gate, preferred_element_type=jnp.float32)]
    reduce_scatter x1 -> x0, waiting for transfers between devices: 28.4 us -> none  [body(): lax.psum_scatter(paired.astype(jnp.bfloat16), 'exp', scatter_dimension=1,...]
    ppermute x2 -> x36, starting transfers between devices: 5.67 us -> 29.4 us  [the longest x16 19.3 us: along_x(): return lax.ppermute(block, 'x', [(i, (i + step) % 4) for i in range(4)])]
    all_gather x1 -> x0, waiting for transfers between devices: 20.4 us -> none  [body(): full_rows = lax.all_gather(h_state, 'exp', axis=1, tiled=True)]
    gather x3 -> x0, local copies, waits for them, and re-layouts: 19 us -> none  [the longest x1 7.49 us: body(): returned[2 * expert_ids, position].astype(jnp.float32)]
  transfers between devices with their start and end apart: 4 -> 36, of which waited for: 2 -> 11; matrix products, arithmetic and copies ran while one was open for 5% -> 4% of each run, Pallas kernels for 0% -> 17%
where the time goes in v1:
time: 232 us; the launch traced here: 231 us
  waiting for transfers between devices  75.3 us (32%)
  Pallas kernels  55.7 us (24%)
  blocking collectives  52.1 us (22%)
  starting transfers between devices  29.4 us (13%)
  local copies, waits for them, and re-layouts  14.7 us (6%)
  other arithmetic  3.45 us (1%)
    ppermute x16, waiting for transfers between devices, along_x(): return lax.ppermute(block, 'x', [(i, (i + step) % 4) for i in range(4)])  74.7 us
    pallas_call x2, Pallas kernels, expert(): pl.pallas_call(expert_kernel, grid_spec=pltpu.PrefetchScalarGridSpec(num_...  40.2 us
    all_to_all x1, blocking collectives, body(): lax.all_to_all(send.reshape(EXPERTS, CAP, QUARTER), ('z', 'y'), split_axi...  31.6 us
    all_to_all x1, blocking collectives, body(): lax.all_to_all(jnp.concatenate(done, axis=0).reshape(EXPERTS, CAP, QUARTE...  20.5 us
    ppermute x16, starting transfers between devices, along_x(): return lax.ppermute(block, 'x', [(i, (i + step) % 4) for i in range(4)])  19.3 us
    pallas_call x1, Pallas kernels, front(): pl.pallas_call(front_kernel, grid_spec=pltpu.PrefetchScalarGridSpec(num_s...  12.2 us
    unnamed x34, local copies, waits for them, and re-layouts  7.46 us
    ppermute x18, starting transfers between devices, other_core(): return lax.ppermute(block, 'c', [(0, 1), (1, 0)])  4.64 us
  transfers between devices with their start and end apart: 36, of which 11 were waited for; matrix products, arithmetic and copies ran while one was open for 4% of the time, Pallas kernels for 17%

profile of v1, /device:TPU:6, one launch (start us, length us, event | category | flops | bytes accessed | tf_op | source)
XLA Modules:
  0.0 231.1 jit_solution(4433261048383409207)
XLA Ops:
  0.0 1.2 slice.114
  1.2 1.8 collective-permute-start
  3.0 0.8 slice_bitcast_fusion.8
  3.8 3.7 %collective-permute-start.1 = (bf16[16,1024]{1,0:T(8,128)(2,1)S(1)}, bf16[16,1024]{1,0:T(8,128)(2,1)S(1)}, u32[]{:S(2)}, u32[]{:S(2)}) collective-permute-start(bf16[16,1024]{1,0:T(8,128)(2,1)S(1)} %slice_bitcast_fusion.8), channel_id=1, source_target_pairs={{0,4},{4,8},{8,12},{12,16},{16,20},{20,24},{24,28},{28,32},{32,36}... | collective-permute-start | bytes 98312 | tf_op jit(solution)/shard_map/ppermute | solution.py:339
  7.5 0.8 copy.16.ids_col
  8.4 1.0 copy-done.3
  9.4 1.0 copy-done.4
  10.3 0.9 copy-done.5
  11.3 0.9 copy-done.6
  12.2 0.9 copy-done.7
  13.2 0.8 copy-done.9
  14.0 12.2 %front.1 = (bf16[256,1024]{1,0:T(8,128)(2,1)S(1)}, bf16[640,1024]{1,0:T(8,128)(2,1)}) custom-call(s32[1]{0:T(128)} %bitcast.x_ref, bf16[3,256,1024]{2,1,0:T(8,128)(2,1)} %proj.1, bf16[2,144,1024]{2,1,0:T(8,128)(2,1)S(1)} %collective-permute-done.halo_kv, bf16[16,1024]{1,0:T(8,128)(2,1)S(1)} %collective-permute-done.1.halo_q, f32[3,3,1024]{2,1,0:T(4,128)S(1)} %copy-done.9, ...), custom_call_target="tpu_custom_call" | custom-call | tf_op jit(solution)/shard_map/front/pallas_call | solution.py:138
  26.2 31.6 %all_to_all.10 = bf16[16,40,1024]{2,1,0:T(8,128)(2,1)S(1)} all-to-all(bf16[16,40,1024]{2,1,0:T(8,128)(2,1)} %bitcast.71), channel_id=1, replica_groups=mesh['z'=4,'y'=4,'c'=2,'x'=4] {'z','y'}, dimensions={0} | all-to-all | bytes 2621440 | tf_op jit(solution)/shard_map/all_to_all | solution.py:344
  57.8 0.1 fusion.8
  57.9 0.9 collective-permute-start.20
  58.8 2.4 %collective-permute-start.19 = (bf16[320,1024]{1,0:T(8,128)(2,1)S(1)}, bf16[320,1024]{1,0:T(8,128)(2,1)S(1)}, u32[]{:S(2)}, u32[]{:S(2)}) collective-permute-start(bf16[320,1024]{1,0:T(8,128)(2,1)S(1)} %bitcast.61), channel_id=1, source_target_pairs={{0,1},{1,2},{2,3},{3,0},{4,5},{5,6},{6,7},{7,4},{8,9},{9,10},{10,1... | collective-permute-start | bytes 1966088 | tf_op jit(solution)/shard_map/ppermute | solution.py:296
  61.3 3.2 %collective-permute-start.2 = (bf16[320,1024]{1,0:T(8,128)(2,1)S(1)}, bf16[320,1024]{1,0:T(8,128)(2,1)S(1)}, u32[]{:S(2)}, u32[]{:S(2)}) collective-permute-start(bf16[320,1024]{1,0:T(8,128)(2,1)S(1)} %bitcast.57), channel_id=1, source_target_pairs={{0,1},{1,2},{2,3},{3,0},{4,5},{5,6},{6,7},{7,4},{8,9},{9,10},{10,1... | collective-permute-start | bytes 1966088 | tf_op jit(solution)/shard_map/ppermute | solution.py:296
  64.5 12.4 %collective-permute-done.20.refs_2_ = bf16[320,1024]{1,0:T(8,128)(2,1)S(1)} collective-permute-done((bf16[320,1024]{1,0:T(8,128)(2,1)S(1)}, bf16[320,1024]{1,0:T(8,128)(2,1)S(1)}, u32[]{:S(2)}, u32[]{:S(2)}) %collective-permute-start.20) | collective-permute-done | bytes 655392 | tf_op jit(solution)/shard_map/ppermute | solution.py:296
  77.0 3.3 %collective-permute-start.21 = (bf16[160,1024]{1,0:T(8,128)(2,1)S(1)}, bf16[160,1024]{1,0:T(8,128)(2,1)S(1)}, u32[]{:S(2)}, u32[]{:S(2)}) collective-permute-start(bf16[160,1024]{1,0:T(8,128)(2,1)S(1)} %slice.162), channel_id=1, source_target_pairs={{0,1},{1,2},{2,3},{3,0},{4,5},{5,6},{6,7},{7,4},{8,9},{9,10},{10,1... | collective-permute-start | bytes 983048 | tf_op jit(solution)/shard_map/ppermute | solution.py:296
  80.3 10.6 %collective-permute-done.3.refs_2_ = bf16[320,1024]{1,0:T(8,128)(2,1)S(1)} collective-permute-done((bf16[320,1024]{1,0:T(8,128)(2,1)S(1)}, bf16[320,1024]{1,0:T(8,128)(2,1)S(1)}, u32[]{:S(2)}, u32[]{:S(2)}) %collective-permute-start.3) | collective-permute-done | bytes 655392 | tf_op jit(solution)/shard_map/ppermute | solution.py:296
  91.0 0.6 collective-permute-start.24
  91.6 2.8 %collective-permute-done.22.refs_4_ = bf16[160,1024]{1,0:T(8,128)(2,1)S(1)} collective-permute-done((bf16[160,1024]{1,0:T(8,128)(2,1)S(1)}, bf16[160,1024]{1,0:T(8,128)(2,1)S(1)}, u32[]{:S(2)}, u32[]{:S(2)}) %collective-permute-start.22) | collective-permute-done | bytes 327712 | tf_op jit(solution)/shard_map/ppermute | solution.py:296
  94.4 0.2 collective-permute-start.4
  94.6 7.8 %collective-permute-done.5.refs_4_ = bf16[160,1024]{1,0:T(8,128)(2,1)S(1)} collective-permute-done((bf16[160,1024]{1,0:T(8,128)(2,1)S(1)}, bf16[160,1024]{1,0:T(8,128)(2,1)S(1)}, u32[]{:S(2)}, u32[]{:S(2)}) %collective-permute-start.5) | collective-permute-done | bytes 327712 | tf_op jit(solution)/shard_map/ppermute | solution.py:296
  102.3 0.6 collective-permute-start.6
  102.9 0.1 collective-permute-start.8
  103.0 0.4 collective-permute-start.7
  103.4 0.5 collective-permute-done.26.refs_8_
  103.9 0.1 collective-permute-start.10
  104.1 0.4 collective-permute-start.9
  104.5 0.5 copy-done.15
  104.9 20.1 %expert.3 = (bf16[4,320,1024]{2,1,0:T(8,128)(2,1)}, bf16[4,320,1024]{2,1,0:T(8,128)(2,1)}) custom-call(s32[1]{0:T(128)} %bitcast.x_ref, bf16[320,1024]{1,0:T(8,128)(2,1)S(1)} %bitcast.63, bf16[320,1024]{1,0:T(8,128)(2,1)S(1)} %collective-permute-done.19.refs_1_, bf16[320,1024]{1,0:T(8,128)(2,1)S(1)} %collective-permute-done.20.refs_2_, ...), custom_call_target="tpu_custom_call" | custom-call | flops 12079595520 | bytes 33554432 | tf_op jit(solution)/shard_map/expert/pallas_call | solution.py:239
  125.0 1.9 slice_bitcast_fusion.3
  127.0 0.5 collective-permute-start.33
  127.5 0.1 collective-permute-start.30
  127.6 0.4 collective-permute-start.29
  128.0 0.5 copy-done.14
  128.4 0.9 copy-done.16
  129.4 20.1 %expert.2 = (bf16[4,320,1024]{2,1,0:T(8,128)(2,1)}, bf16[4,320,1024]{2,1,0:T(8,128)(2,1)}) custom-call(s32[1]{0:T(128)} %bitcast.x_ref, bf16[320,1024]{1,0:T(8,128)(2,1)S(1)} %bitcast.59, bf16[320,1024]{1,0:T(8,128)(2,1)S(1)} %collective-permute-done.2.refs_1_, bf16[320,1024]{1,0:T(8,128)(2,1)S(1)} %collective-permute-done.3.refs_2_, ...), custom_call_target="tpu_custom_call" | custom-call | flops 12079595520 | bytes 33554432 | tf_op jit(solution)/shard_map/expert/pallas_call | solution.py:239
  149.5 2.1 slice_bitcast_fusion.7
  151.6 0.5 collective-permute-start.16
  152.1 0.1 collective-permute-start.13
  152.2 0.4 collective-permute-start.12
  152.6 0.1 collective-permute-start.28
  152.7 0.4 collective-permute-start.11
  153.1 0.9 fusion.2
  154.1 2.4 %collective-permute-start.31 = (bf16[160,1024]{1,0:T(8,128)(2,1)S(1)}, bf16[160,1024]{1,0:T(8,128)(2,1)S(1)}, u32[]{:S(2)}, u32[]{:S(2)}) collective-permute-start(bf16[160,1024]{1,0:T(8,128)(2,1)S(1)} %get-tuple-element.35), channel_id=1, source_target_pairs={{0,1},{1,2},{2,3},{3,0},{4,5},{5,6},{6,7},{7,4},{8,9},{9,10},{10,1... | collective-permute-start | bytes 983048 | tf_op jit(solution)/shard_map/ppermute | solution.py:296
  156.6 0.9 fusion.6
  157.6 3.3 %collective-permute-start.14 = (bf16[160,1024]{1,0:T(8,128)(2,1)S(1)}, bf16[160,1024]{1,0:T(8,128)(2,1)S(1)}, u32[]{:S(2)}, u32[]{:S(2)}) collective-permute-start(bf16[160,1024]{1,0:T(8,128)(2,1)S(1)} %get-tuple-element.33), channel_id=1, source_target_pairs={{0,1},{1,2},{2,3},{3,0},{4,5},{5,6},{6,7},{7,4},{8,9},{9,10},{10,1... | collective-permute-start | bytes 983048 | tf_op jit(solution)/shard_map/ppermute | solution.py:296
  160.9 6.6 %collective-permute-done.34 = bf16[160,1024]{1,0:T(8,128)(2,1)S(1)} collective-permute-done((bf16[160,1024]{1,0:T(8,128)(2,1)S(1)}, bf16[160,1024]{1,0:T(8,128)(2,1)S(1)}, u32[]{:S(2)}, u32[]{:S(2)}) %collective-permute-start.34) | collective-permute-done | bytes 327712 | tf_op jit(solution)/shard_map/ppermute | solution.py:296
  167.5 0.1 add_convert_fusion.2
  167.8 0.1 add_convert_fusion.3
  167.9 11.4 %collective-permute-done.17 = bf16[160,1024]{1,0:T(8,128)(2,1)S(1)} collective-permute-done((bf16[160,1024]{1,0:T(8,128)(2,1)S(1)}, bf16[160,1024]{1,0:T(8,128)(2,1)S(1)}, u32[]{:S(2)}, u32[]{:S(2)}) %collective-permute-start.17) | collective-permute-done | bytes 327712 | tf_op jit(solution)/shard_map/ppermute | solution.py:296
  179.4 0.1 add_convert_fusion.4
  179.6 2.1 collective-permute-start.18
  181.8 1.3 collective-permute-start.15
  183.1 10.3 %collective-permute-done.35 = bf16[320,1024]{1,0:T(8,128)(2,1)S(1)} collective-permute-done((bf16[320,1024]{1,0:T(8,128)(2,1)S(1)}, bf16[320,1024]{1,0:T(8,128)(2,1)S(1)}, u32[]{:S(2)}, u32[]{:S(2)}) %collective-permute-start.35) | collective-permute-done | bytes 655392 | tf_op jit(solution)/shard_map/ppermute | solution.py:296
  193.4 3.6 %collective-permute-done.32 = bf16[320,1024]{1,0:T(8,128)(2,1)S(1)} collective-permute-done((bf16[320,1024]{1,0:T(8,128)(2,1)S(1)}, bf16[320,1024]{1,0:T(8,128)(2,1)S(1)}, u32[]{:S(2)}, u32[]{:S(2)}) %collective-permute-start.32) | collective-permute-done | bytes 655392 | tf_op jit(solution)/shard_map/ppermute | solution.py:296
  197.1 0.5 add_convert_fusion
  197.6 8.2 %collective-permute-done.18 = bf16[320,1024]{1,0:T(8,128)(2,1)S(1)} collective-permute-done((bf16[320,1024]{1,0:T(8,128)(2,1)S(1)}, bf16[320,1024]{1,0:T(8,128)(2,1)S(1)}, u32[]{:S(2)}, u32[]{:S(2)}) %collective-permute-start.18) | collective-permute-done | bytes 655392 | tf_op jit(solution)/shard_map/ppermute | solution.py:296
  205.8 1.0 collective-permute-done.15
  206.8 0.5 add_convert_fusion.1
  207.4 20.5 %all_to_all.11 = bf16[16,40,1024]{2,1,0:T(8,128)(2,1)S(1)} all-to-all(bf16[16,40,1024]{2,1,0:T(8,128)(2,1)S(1)} %bitcast.70), channel_id=1, replica_groups=mesh['z'=4,'y'=4,'c'=2,'x'=4] {'z','y'}, dimensions={0} | all-to-all | bytes 2621440 | tf_op jit(solution)/shard_map/all_to_all | solution.py:354
  227.8 3.3 %finish.1 = bf16[256,1024]{1,0:T(8,128)(2,1)} custom-call(bf16[256,1024]{1,0:T(8,128)(2,1)S(1)} %get-tuple-element.11.h, bf16[640,1024]{1,0:T(8,128)(2,1)S(1)} %bitcast.55, s32[256,1]{1,0:T(8,128)S(1)} %copy.16.ids_col, s32[1,256]{1,0:T(1,128)S(1)} %bitcast.69), custom_call_target="tpu_custom_call" | custom-call | tf_op jit(solution)/shard_map/finish/pallas_call | solution.py:279
  (78 shorter events, 1.0 us)
Async XLA Ops:
  0.0 8.4 %copy-start.2 = (bf16[400,384]{1,0:T(8,128)(2,1)S(1)}, bf16[400,384]{1,0:T(8,128)(2,1)}, u32[]{:S(2)}) copy-start(bf16[400,384]{1,0:T(8,128)(2,1)} %constant.20.clone.fwd3) | copy-start | bytes 921604
  0.0 8.4 %copy-start.10 = (s32[256]{0:T(256)S(1)}, s32[256]{0:T(256)}, u32[]{:S(2)}) copy-start(s32[256]{0:T(256)} %param.20) | copy-start | bytes 3076
  0.0 8.4 %copy-start.8 = (f32[4096]{0:T(1024)S(1)}, f32[4096]{0:T(1024)}, u32[]{:S(2)}) copy-start(f32[4096]{0:T(1024)} %param.19) | copy-start | bytes 49156
  0.0 8.4 %copy-start.1 = (bf16[256,1024]{1,0:T(8,128)(2,1)S(1)}, bf16[256,1024]{1,0:T(8,128)(2,1)}, u32[]{:S(2)}) copy-start(bf16[256,1024]{1,0:T(8,128)(2,1)} %res.1) | copy-start | bytes 1572868
  0.0 8.4 %copy-start = (f32[128,1024]{1,0:T(8,128)S(1)}, f32[128,1024]{1,0:T(8,128)}, u32[]{:S(2)}) copy-start(f32[128,1024]{1,0:T(8,128)} %long_f.1) | copy-start | bytes 1572868
  1.2 7.1 %collective-permute-start = (bf16[2,144,1024]{2,1,0:T(8,128)(2,1)S(1)}, bf16[2,144,1024]{2,1,0:T(8,128)(2,1)S(1)}, u32[]{:S(2)}, u32[]{:S(2)}) collective-permute-start(bf16[2,144,1024]{2,1,0:T(8,128)(2,1)S(1)} %slice.114), channel_id=1, source_target_pairs={{0,4},{4,8},{8,12},{12,16},{16,20},{20,24},{24,28},{28,32},{32,36}... | collective-permute-start | bytes 1769480 | tf_op jit(solution)/shard_map/ppermute | solution.py:338
  3.8 4.6 %collective-permute-start.1 = (bf16[16,1024]{1,0:T(8,128)(2,1)S(1)}, bf16[16,1024]{1,0:T(8,128)(2,1)S(1)}, u32[]{:S(2)}, u32[]{:S(2)}) collective-permute-start(bf16[16,1024]{1,0:T(8,128)(2,1)S(1)} %slice_bitcast_fusion.8), channel_id=1, source_target_pairs={{0,4},{4,8},{8,12},{12,16},{16,20},{20,24},{24,28},{28,32},{32,36}... | collective-permute-start | bytes 98312 | tf_op jit(solution)/shard_map/ppermute | solution.py:339
  8.4 1.0 copy-start.3
  9.4 1.0 copy-start.4
  10.3 0.9 copy-start.5
  11.3 0.9 copy-start.6
  12.2 0.9 copy-start.7
  13.2 0.8 copy-start.9
  57.9 19.0 %collective-permute-start.20 = (bf16[320,1024]{1,0:T(8,128)(2,1)S(1)}, bf16[320,1024]{1,0:T(8,128)(2,1)S(1)}, u32[]{:S(2)}, u32[]{:S(2)}) collective-permute-start(bf16[320,1024]{1,0:T(8,128)(2,1)S(1)} %bitcast.60), channel_id=1, source_target_pairs={{0,3},{1,0},{2,1},{3,2},{4,7},{5,4},{6,5},{7,6},{8,11},{9,8},{10,9... | collective-permute-start | bytes 1966088 | tf_op jit(solution)/shard_map/ppermute | solution.py:296
  58.8 18.2 %collective-permute-start.19 = (bf16[320,1024]{1,0:T(8,128)(2,1)S(1)}, bf16[320,1024]{1,0:T(8,128)(2,1)S(1)}, u32[]{:S(2)}, u32[]{:S(2)}) collective-permute-start(bf16[320,1024]{1,0:T(8,128)(2,1)S(1)} %bitcast.61), channel_id=1, source_target_pairs={{0,1},{1,2},{2,3},{3,0},{4,5},{5,6},{6,7},{7,4},{8,9},{9,10},{10,1... | collective-permute-start | bytes 1966088 | tf_op jit(solution)/shard_map/ppermute | solution.py:296
  61.2 29.6 %collective-permute-start.3 = (bf16[320,1024]{1,0:T(8,128)(2,1)S(1)}, bf16[320,1024]{1,0:T(8,128)(2,1)S(1)}, u32[]{:S(2)}, u32[]{:S(2)}) collective-permute-start(bf16[320,1024]{1,0:T(8,128)(2,1)S(1)} %bitcast.56), channel_id=1, source_target_pairs={{0,3},{1,0},{2,1},{3,2},{4,7},{5,4},{6,5},{7,6},{8,11},{9,8},{10,9... | collective-permute-start | bytes 1966088 | tf_op jit(solution)/shard_map/ppermute | solution.py:296
  61.2 29.7 %collective-permute-start.23 = (bf16[320,1024]{1,0:T(8,128)(2,1)S(1)}, bf16[320,1024]{1,0:T(8,128)(2,1)S(1)}, u32[]{:S(2)}, u32[]{:S(2)}) collective-permute-start(bf16[320,1024]{1,0:T(8,128)(2,1)S(1)} %bitcast.62), channel_id=1, source_target_pairs={{0,4},{4,0},{1,5},{5,1},{2,6},{6,2},{3,7},{7,3},{8,12},{12,8},{9,1... | collective-permute-start | bytes 1966088 | tf_op jit(solution)/shard_map/ppermute | solution.py:300
  61.3 29.7 %collective-permute-start.2 = (bf16[320,1024]{1,0:T(8,128)(2,1)S(1)}, bf16[320,1024]{1,0:T(8,128)(2,1)S(1)}, u32[]{:S(2)}, u32[]{:S(2)}) collective-permute-start(bf16[320,1024]{1,0:T(8,128)(2,1)S(1)} %bitcast.57), channel_id=1, source_target_pairs={{0,1},{1,2},{2,3},{3,0},{4,5},{5,6},{6,7},{7,4},{8,9},{9,10},{10,1... | collective-permute-start | bytes 1966088 | tf_op jit(solution)/shard_map/ppermute | solution.py:296
  76.9 17.5 %collective-permute-start.22 = (bf16[160,1024]{1,0:T(8,128)(2,1)S(1)}, bf16[160,1024]{1,0:T(8,128)(2,1)S(1)}, u32[]{:S(2)}, u32[]{:S(2)}) collective-permute-start(bf16[160,1024]{1,0:T(8,128)(2,1)S(1)} %slice.163), channel_id=1, source_target_pairs={{0,3},{1,0},{2,1},{3,2},{4,7},{5,4},{6,5},{7,6},{8,11},{9,8},{10,9... | collective-permute-start | bytes 983048 | tf_op jit(solution)/shard_map/ppermute | solution.py:296
  77.0 17.5 %collective-permute-start.21 = (bf16[160,1024]{1,0:T(8,128)(2,1)S(1)}, bf16[160,1024]{1,0:T(8,128)(2,1)S(1)}, u32[]{:S(2)}, u32[]{:S(2)}) collective-permute-start(bf16[160,1024]{1,0:T(8,128)(2,1)S(1)} %slice.162), channel_id=1, source_target_pairs={{0,1},{1,2},{2,3},{3,0},{4,5},{5,6},{6,7},{7,4},{8,9},{9,10},{10,1... | collective-permute-start | bytes 983048 | tf_op jit(solution)/shard_map/ppermute | solution.py:296
  90.9 12.2 %collective-permute-start.25 = (bf16[320,1024]{1,0:T(8,128)(2,1)S(1)}, bf16[320,1024]{1,0:T(8,128)(2,1)S(1)}, u32[]{:S(2)}, u32[]{:S(2)}) collective-permute-start(bf16[320,1024]{1,0:T(8,128)(2,1)S(1)} %collective-permute-done.20.refs_2_), channel_id=1, source_target_pairs={{0,4},{4,0},{1,5},{5,1},{2,6},{6,2},{3,7},{7,3},{8,12},{12,8},{9,1... | collective-permute-start | bytes 1966088 | tf_op jit(solution)/shard_map/ppermute | solution.py:300
  90.9 11.4 %collective-permute-start.5 = (bf16[160,1024]{1,0:T(8,128)(2,1)S(1)}, bf16[160,1024]{1,0:T(8,128)(2,1)S(1)}, u32[]{:S(2)}, u32[]{:S(2)}) collective-permute-start(bf16[160,1024]{1,0:T(8,128)(2,1)S(1)} %slice.154), channel_id=1, source_target_pairs={{0,3},{1,0},{2,1},{3,2},{4,7},{5,4},{6,5},{7,6},{8,11},{9,8},{10,9... | collective-permute-start | bytes 983048 | tf_op jit(solution)/shard_map/ppermute | solution.py:296
  91.0 13.1 %collective-permute-start.24 = (bf16[320,1024]{1,0:T(8,128)(2,1)S(1)}, bf16[320,1024]{1,0:T(8,128)(2,1)S(1)}, u32[]{:S(2)}, u32[]{:S(2)}) collective-permute-start(bf16[320,1024]{1,0:T(8,128)(2,1)S(1)} %collective-permute-done.19.refs_1_), channel_id=1, source_target_pairs={{0,4},{4,0},{1,5},{5,1},{2,6},{6,2},{3,7},{7,3},{8,12},{12,8},{9,1... | collective-permute-start | bytes 1966088 | tf_op jit(solution)/shard_map/ppermute | solution.py:300
  94.4 7.9 %collective-permute-start.4 = (bf16[160,1024]{1,0:T(8,128)(2,1)S(1)}, bf16[160,1024]{1,0:T(8,128)(2,1)S(1)}, u32[]{:S(2)}, u32[]{:S(2)}) collective-permute-start(bf16[160,1024]{1,0:T(8,128)(2,1)S(1)} %slice.153), channel_id=1, source_target_pairs={{0,1},{1,2},{2,3},{3,0},{4,5},{5,6},{6,7},{7,4},{8,9},{9,10},{10,1... | collective-permute-start | bytes 983048 | tf_op jit(solution)/shard_map/ppermute | solution.py:296
  94.6 8.4 %collective-permute-start.27 = (bf16[160,1024]{1,0:T(8,128)(2,1)S(1)}, bf16[160,1024]{1,0:T(8,128)(2,1)S(1)}, u32[]{:S(2)}, u32[]{:S(2)}) collective-permute-start(bf16[160,1024]{1,0:T(8,128)(2,1)S(1)} %collective-permute-done.22.refs_4_), channel_id=1, source_target_pairs={{0,4},{4,0},{1,5},{5,1},{2,6},{6,2},{3,7},{7,3},{8,12},{12,8},{9,1... | collective-permute-start | bytes 983048 | tf_op jit(solution)/shard_map/ppermute | solution.py:300
  102.3 1.6 collective-permute-start.26
  102.3 24.6 %collective-permute-start.6 = (bf16[320,1024]{1,0:T(8,128)(2,1)S(1)}, bf16[320,1024]{1,0:T(8,128)(2,1)S(1)}, u32[]{:S(2)}, u32[]{:S(2)}) collective-permute-start(bf16[320,1024]{1,0:T(8,128)(2,1)S(1)} %bitcast.58), channel_id=1, source_target_pairs={{0,4},{4,0},{1,5},{5,1},{2,6},{6,2},{3,7},{7,3},{8,12},{12,8},{9,1... | collective-permute-start | bytes 1966088 | tf_op jit(solution)/shard_map/ppermute | solution.py:300
  102.9 24.7 %collective-permute-start.8 = (bf16[320,1024]{1,0:T(8,128)(2,1)S(1)}, bf16[320,1024]{1,0:T(8,128)(2,1)S(1)}, u32[]{:S(2)}, u32[]{:S(2)}) collective-permute-start(bf16[320,1024]{1,0:T(8,128)(2,1)S(1)} %collective-permute-done.3.refs_2_), channel_id=1, source_target_pairs={{0,4},{4,0},{1,5},{5,1},{2,6},{6,2},{3,7},{7,3},{8,12},{12,8},{9,1... | collective-permute-start | bytes 1966088 | tf_op jit(solution)/shard_map/ppermute | solution.py:300
  103.0 1.4 copy-start.13
  103.0 25.0 %collective-permute-start.7 = (bf16[320,1024]{1,0:T(8,128)(2,1)S(1)}, bf16[320,1024]{1,0:T(8,128)(2,1)S(1)}, u32[]{:S(2)}, u32[]{:S(2)}) collective-permute-start(bf16[320,1024]{1,0:T(8,128)(2,1)S(1)} %collective-permute-done.2.refs_1_), channel_id=1, source_target_pairs={{0,4},{4,0},{1,5},{5,1},{2,6},{6,2},{3,7},{7,3},{8,12},{12,8},{9,1... | collective-permute-start | bytes 1966088 | tf_op jit(solution)/shard_map/ppermute | solution.py:300
  103.9 23.5 %collective-permute-start.10 = (bf16[160,1024]{1,0:T(8,128)(2,1)S(1)}, bf16[160,1024]{1,0:T(8,128)(2,1)S(1)}, u32[]{:S(2)}, u32[]{:S(2)}) collective-permute-start(bf16[160,1024]{1,0:T(8,128)(2,1)S(1)} %collective-permute-done.5.refs_4_), channel_id=1, source_target_pairs={{0,4},{4,0},{1,5},{5,1},{2,6},{6,2},{3,7},{7,3},{8,12},{12,8},{9,1... | collective-permute-start | bytes 983048 | tf_op jit(solution)/shard_map/ppermute | solution.py:300
  104.1 0.9 copy-start.15
  104.1 23.9 %collective-permute-start.9 = (bf16[160,1024]{1,0:T(8,128)(2,1)S(1)}, bf16[160,1024]{1,0:T(8,128)(2,1)S(1)}, u32[]{:S(2)}, u32[]{:S(2)}) collective-permute-start(bf16[160,1024]{1,0:T(8,128)(2,1)S(1)} %collective-permute-done.4.refs_3_), channel_id=1, source_target_pairs={{0,4},{4,0},{1,5},{5,1},{2,6},{6,2},{3,7},{7,3},{8,12},{12,8},{9,1... | collective-permute-start | bytes 983048 | tf_op jit(solution)/shard_map/ppermute | solution.py:300
  127.0 25.2 %collective-permute-start.33 = (bf16[320,1024]{1,0:T(8,128)(2,1)S(1)}, bf16[320,1024]{1,0:T(8,128)(2,1)S(1)}, u32[]{:S(2)}, u32[]{:S(2)}) collective-permute-start(bf16[320,1024]{1,0:T(8,128)(2,1)S(1)} %get-tuple-element.25), channel_id=1, source_target_pairs={{0,4},{4,0},{1,5},{5,1},{2,6},{6,2},{3,7},{7,3},{8,12},{12,8},{9,1... | collective-permute-start | bytes 1966088 | tf_op jit(solution)/shard_map/ppermute | solution.py:300
  127.5 25.1 %collective-permute-start.30 = (bf16[320,1024]{1,0:T(8,128)(2,1)S(1)}, bf16[320,1024]{1,0:T(8,128)(2,1)S(1)}, u32[]{:S(2)}, u32[]{:S(2)}) collective-permute-start(bf16[320,1024]{1,0:T(8,128)(2,1)S(1)} %get-tuple-element.26), channel_id=1, source_target_pairs={{0,4},{4,0},{1,5},{5,1},{2,6},{6,2},{3,7},{7,3},{8,12},{12,8},{9,1... | collective-permute-start | bytes 1966088 | tf_op jit(solution)/shard_map/ppermute | solution.py:300
  127.6 0.8 copy-start.14
  127.6 25.1 %collective-permute-start.29 = (bf16[320,1024]{1,0:T(8,128)(2,1)S(1)}, bf16[320,1024]{1,0:T(8,128)(2,1)S(1)}, u32[]{:S(2)}, u32[]{:S(2)}) collective-permute-start(bf16[320,1024]{1,0:T(8,128)(2,1)S(1)} %get-tuple-element.27), channel_id=1, source_target_pairs={{0,4},{4,0},{1,5},{5,1},{2,6},{6,2},{3,7},{7,3},{8,12},{12,8},{9,1... | collective-permute-start | bytes 1966088 | tf_op jit(solution)/shard_map/ppermute | solution.py:300
  128.4 0.9 copy-start.16
  149.5 3.6 %copy-start.11 = (bf16[4,320,1024]{2,1,0:T(8,128)(2,1)S(1)}, bf16[4,320,1024]{2,1,0:T(8,128)(2,1)}, u32[]{:S(2)}) copy-start(bf16[4,320,1024]{2,1,0:T(8,128)(2,1)} %get-tuple-element.15) | copy-start | bytes 7864324
  151.6 2.5 %collective-permute-start.16 = (bf16[320,1024]{1,0:T(8,128)(2,1)S(1)}, bf16[320,1024]{1,0:T(8,128)(2,1)S(1)}, u32[]{:S(2)}, u32[]{:S(2)}) collective-permute-start(bf16[320,1024]{1,0:T(8,128)(2,1)S(1)} %get-tuple-element.18), channel_id=1, source_target_pairs={{0,4},{4,0},{1,5},{5,1},{2,6},{6,2},{3,7},{7,3},{8,12},{12,8},{9,1... | collective-permute-start | bytes 1966088 | tf_op jit(solution)/shard_map/ppermute | solution.py:300
  152.1 4.5 %collective-permute-start.13 = (bf16[320,1024]{1,0:T(8,128)(2,1)S(1)}, bf16[320,1024]{1,0:T(8,128)(2,1)S(1)}, u32[]{:S(2)}, u32[]{:S(2)}) collective-permute-start(bf16[320,1024]{1,0:T(8,128)(2,1)S(1)} %get-tuple-element.19), channel_id=1, source_target_pairs={{0,4},{4,0},{1,5},{5,1},{2,6},{6,2},{3,7},{7,3},{8,12},{12,8},{9,1... | collective-permute-start | bytes 1966088 | tf_op jit(solution)/shard_map/ppermute | solution.py:300
  152.2 4.4 %collective-permute-start.12 = (bf16[320,1024]{1,0:T(8,128)(2,1)S(1)}, bf16[320,1024]{1,0:T(8,128)(2,1)S(1)}, u32[]{:S(2)}, u32[]{:S(2)}) collective-permute-start(bf16[320,1024]{1,0:T(8,128)(2,1)S(1)} %get-tuple-element.20), channel_id=1, source_target_pairs={{0,4},{4,0},{1,5},{5,1},{2,6},{6,2},{3,7},{7,3},{8,12},{12,8},{9,1... | collective-permute-start | bytes 1966088 | tf_op jit(solution)/shard_map/ppermute | solution.py:300
  152.6 29.2 %collective-permute-start.28 = (bf16[320,1024]{1,0:T(8,128)(2,1)S(1)}, bf16[320,1024]{1,0:T(8,128)(2,1)S(1)}, u32[]{:S(2)}, u32[]{:S(2)}) collective-permute-start(bf16[320,1024]{1,0:T(8,128)(2,1)S(1)} %get-tuple-element.24), channel_id=1, source_target_pairs={{0,4},{4,0},{1,5},{5,1},{2,6},{6,2},{3,7},{7,3},{8,12},{12,8},{9,1... | collective-permute-start | bytes 1966088 | tf_op jit(solution)/shard_map/ppermute | solution.py:300
  152.7 44.8 %collective-permute-start.11 = (bf16[320,1024]{1,0:T(8,128)(2,1)S(1)}, bf16[320,1024]{1,0:T(8,128)(2,1)S(1)}, u32[]{:S(2)}, u32[]{:S(2)}) collective-permute-start(bf16[320,1024]{1,0:T(8,128)(2,1)S(1)} %get-tuple-element.17), channel_id=1, source_target_pairs={{0,4},{4,0},{1,5},{5,1},{2,6},{6,2},{3,7},{7,3},{8,12},{12,8},{9,1... | collective-permute-start | bytes 1966088 | tf_op jit(solution)/shard_map/ppermute | solution.py:300
  154.0 2.6 %copy-start.12 = (bf16[4,320,1024]{2,1,0:T(8,128)(2,1)S(1)}, bf16[4,320,1024]{2,1,0:T(8,128)(2,1)}, u32[]{:S(2)}) copy-start(bf16[4,320,1024]{2,1,0:T(8,128)(2,1)} %get-tuple-element.13) | copy-start | bytes 7864324
  154.1 13.6 %collective-permute-start.31 = (bf16[160,1024]{1,0:T(8,128)(2,1)S(1)}, bf16[160,1024]{1,0:T(8,128)(2,1)S(1)}, u32[]{:S(2)}, u32[]{:S(2)}) collective-permute-start(bf16[160,1024]{1,0:T(8,128)(2,1)S(1)} %get-tuple-element.35), channel_id=1, source_target_pairs={{0,1},{1,2},{2,3},{3,0},{4,5},{5,6},{6,7},{7,4},{8,9},{9,10},{10,1... | collective-permute-start | bytes 983048 | tf_op jit(solution)/shard_map/ppermute | solution.py:296
  156.6 11.0 %collective-permute-start.34 = (bf16[160,1024]{1,0:T(8,128)(2,1)S(1)}, bf16[160,1024]{1,0:T(8,128)(2,1)S(1)}, u32[]{:S(2)}, u32[]{:S(2)}) collective-permute-start(bf16[160,1024]{1,0:T(8,128)(2,1)S(1)} %get-tuple-element.36), channel_id=1, source_target_pairs={{0,3},{1,0},{2,1},{3,2},{4,7},{5,4},{6,5},{7,6},{8,11},{9,8},{10,9... | collective-permute-start | bytes 983048 | tf_op jit(solution)/shard_map/ppermute | solution.py:296
  157.6 22.0 %collective-permute-start.14 = (bf16[160,1024]{1,0:T(8,128)(2,1)S(1)}, bf16[160,1024]{1,0:T(8,128)(2,1)S(1)}, u32[]{:S(2)}, u32[]{:S(2)}) collective-permute-start(bf16[160,1024]{1,0:T(8,128)(2,1)S(1)} %get-tuple-element.33), channel_id=1, source_target_pairs={{0,1},{1,2},{2,3},{3,0},{4,5},{5,6},{6,7},{7,4},{8,9},{9,10},{10,1... | collective-permute-start | bytes 983048 | tf_op jit(solution)/shard_map/ppermute | solution.py:296
  167.5 11.9 %collective-permute-start.17 = (bf16[160,1024]{1,0:T(8,128)(2,1)S(1)}, bf16[160,1024]{1,0:T(8,128)(2,1)S(1)}, u32[]{:S(2)}, u32[]{:S(2)}) collective-permute-start(bf16[160,1024]{1,0:T(8,128)(2,1)S(1)} %get-tuple-element.34), channel_id=1, source_target_pairs={{0,3},{1,0},{2,1},{3,2},{4,7},{5,4},{6,5},{7,6},{8,11},{9,8},{10,9... | collective-permute-start | bytes 983048 | tf_op jit(solution)/shard_map/ppermute | solution.py:296
  167.7 25.7 %collective-permute-start.35 = (bf16[320,1024]{1,0:T(8,128)(2,1)S(1)}, bf16[320,1024]{1,0:T(8,128)(2,1)S(1)}, u32[]{:S(2)}, u32[]{:S(2)}) collective-permute-start(bf16[320,1024]{1,0:T(8,128)(2,1)S(1)} %pad_maximum_fusion.4), channel_id=1, source_target_pairs={{0,3},{1,0},{2,1},{3,2},{4,7},{5,4},{6,5},{7,6},{8,11},{9,8},{10,9... | collective-permute-start | bytes 1966088 | tf_op jit(solution)/shard_map/ppermute | solution.py:296
  179.4 17.7 %collective-permute-start.32 = (bf16[320,1024]{1,0:T(8,128)(2,1)S(1)}, bf16[320,1024]{1,0:T(8,128)(2,1)S(1)}, u32[]{:S(2)}, u32[]{:S(2)}) collective-permute-start(bf16[320,1024]{1,0:T(8,128)(2,1)S(1)} %pad_maximum_fusion.3), channel_id=1, source_target_pairs={{0,1},{1,2},{2,3},{3,0},{4,5},{5,6},{6,7},{7,4},{8,9},{9,10},{10,1... | collective-permute-start | bytes 1966088 | tf_op jit(solution)/shard_map/ppermute | solution.py:296
  179.6 26.2 %collective-permute-start.18 = (bf16[320,1024]{1,0:T(8,128)(2,1)S(1)}, bf16[320,1024]{1,0:T(8,128)(2,1)S(1)}, u32[]{:S(2)}, u32[]{:S(2)}) collective-permute-start(bf16[320,1024]{1,0:T(8,128)(2,1)S(1)} %pad_maximum_fusion.2), channel_id=1, source_target_pairs={{0,3},{1,0},{2,1},{3,2},{4,7},{5,4},{6,5},{7,6},{8,11},{9,8},{10,9... | collective-permute-start | bytes 1966088 | tf_op jit(solution)/shard_map/ppermute | solution.py:296
  181.8 24.9 %collective-permute-start.15 = (bf16[320,1024]{1,0:T(8,128)(2,1)S(1)}, bf16[320,1024]{1,0:T(8,128)(2,1)S(1)}, u32[]{:S(2)}, u32[]{:S(2)}) collective-permute-start(bf16[320,1024]{1,0:T(8,128)(2,1)S(1)} %pad_maximum_fusion.1), channel_id=1, source_target_pairs={{0,1},{1,2},{2,3},{3,0},{4,5},{5,6},{6,7},{7,4},{8,9},{9,10},{10,1... | collective-permute-start | bytes 1966088 | tf_op jit(solution)/shard_map/ppermute | solution.py:296
